TPU v7x, 256 devices: a whole 4x4x8 slice. The times are simulated.
256 devices in a mesh: seq: 64 (over z, x, core), tp: 4 (over y).
Axes of the slice: x: 4, y: 4, z: 8, core: 2. Of those that a mesh axis runs over, the one named last changes fastest.
Arguments:
- query: bfloat16 [32768, 2048], P('seq', 'tp'), may hold values from -6 to 6
- keys: bfloat16 [32768, 2048], P('seq', 'tp'), may hold values from -6 to 6
- values: bfloat16 [32768, 2048], P('seq', 'tp'), may hold values from -7 to 7
- beta: float32 [16], P('tp'), may hold values from -2 to 2
- out_weight: bfloat16 [2048, 2048], P('tp'), may hold values from -0.125 to 0.125
- cotangent: bfloat16 [32768, 2048], P(('seq', 'tp')), may hold values from -6 to 6
Outputs:
- output: bfloat16 [32768, 2048], P(('seq', 'tp'))
- grad_query: bfloat16 [32768, 2048], P('seq', 'tp')
- grad_keys: bfloat16 [32768, 2048], P('seq', 'tp')
- grad_values: bfloat16 [32768, 2048], P('seq', 'tp')
All inputs are finite; a program needn't handle non-finite values.
Results may differ from a plain program's by a relative error of at most 0.0055.
The roundings to bfloat16 on the way count: a program that leaves them out, or rounds other values in their place, can miss the bound.
Values may be sent and summed in bfloat16 or wider, within the bound.
A program may use at most 128 MiB of HBM per device.

v0:
```python
import jax
import jax.numpy as jnp
from jax import lax
from jax.sharding import Mesh
from jax.sharding import PartitionSpec as P

HD = 128
SEQ = ("seq_0", "seq_1", "seq_2")
SEQ_TP = ("seq_0", "seq_1", "seq_2", "tp")


precise = lax.Precision.HIGH


def nothing_yet(shard, identity):
    return jax.tree.map(
        lambda a, e: jnp.broadcast_to(jnp.asarray(e, a.dtype), a.shape), shard, identity
    )


def prefix_by_axis(shard, axes, combine, identity, reverse):
    before = start = nothing_yet(shard, identity)
    total = shard
    for axis in reversed(axes):
        peers, index = (lax.axis_size(axis), lax.axis_index(axis))
        pieces = jax.tree.map(
            lambda part, kind: lax.all_gather(part.astype(kind), axis),
            total,
            (jnp.bfloat16, jnp.bfloat16),
        )
        inside, total = (start, start)
        for k in reversed(range(peers)) if reverse else range(peers):
            passed = k > index if reverse else k < index
            total = combine(
                total, jax.tree.map(lambda part, own: part[k].astype(own.dtype), pieces, shard)
            )
            inside = jax.tree.map(lambda new, old: jnp.where(passed, new, old), total, inside)
        before = combine(inside, before)
    return before


def cut_along(shard, dim, peers):
    dims = shard.shape
    blocks = shard.reshape(*dims[:dim], peers, dims[dim] // peers, *dims[dim + 1 :])
    return jnp.moveaxis(blocks, dim, 0)


def sent_and_summed(shard, axis, dim):
    peers = lax.axis_size(axis)
    blocks = lax.all_to_all(cut_along(shard, dim, peers), axis, 0, 0, tiled=True)
    return jnp.sum(blocks, axis=0)


def sent_to_all(shard, axis):
    peers = lax.axis_size(axis)
    return lax.all_to_all(
        jnp.broadcast_to(shard[None], (peers, *shard.shape)), axis, 0, 0, tiled=True
    )


def laid_out(blocks, dim):
    dims = list(blocks.shape[1:])
    dims[dim] *= blocks.shape[0]
    return jnp.moveaxis(blocks, 0, dim).reshape(dims)


def gathered_copies(shard, axis, dim):
    blocks = sent_to_all(shard, axis)
    return laid_out(blocks, dim)


def plus_one(inputs):
    return jnp.where(inputs > 0, inputs + 1.0, jnp.exp(jnp.minimum(inputs, 0.0)))


def slope_of(inputs):
    return jnp.where(inputs > 0, jnp.ones_like(inputs), jnp.exp(jnp.minimum(inputs, 0.0)))


def add_pair(earlier, later):
    return (earlier[0] + later[0], earlier[1] + later[1])


def local(query, keys, values, beta, out_weight, cotangent):
    length = query.shape[0]
    width = query.shape[1]
    local_heads = width // HD
    scale_factor = HD ** (-0.5)

    def shaped(tensor):
        return tensor.reshape(length, local_heads, HD)

    query_h, keys_h, values_h = (shaped(query), shaped(keys), shaped(values))
    gate_mix = jax.nn.sigmoid(beta)[None, :, None]
    query_f = query_h.astype(jnp.float32)
    keys_f = keys_h.astype(jnp.float32)
    query_feat = plus_one(query_f)
    key_feat = plus_one(keys_f)
    own_memory = jnp.einsum(
        "lhc,lhd->hcd", key_feat, values_h, precision=precise, preferred_element_type=jnp.float32
    )
    own_sum = jnp.sum(key_feat, 0)
    memory, memory_sum = prefix_by_axis(
        (own_memory, own_sum),
        SEQ,
        add_pair,
        (jnp.zeros_like(own_memory), jnp.zeros_like(own_sum)),
        False,
    )
    causal = jnp.arange(length)[:, None] >= jnp.arange(length)[None, :]
    scores = (
        jnp.einsum("lhc,mhc->hlm", query_h, keys_h, preferred_element_type=jnp.float32)
        * scale_factor
    )
    scores = jnp.where(causal[None], scores, -jnp.inf)
    top_score = jnp.max(scores, -1, keepdims=True)
    expo = jnp.exp(scores - top_score)
    probs = expo / jnp.sum(expo, -1, keepdims=True)
    probs_b = probs.astype(jnp.bfloat16)
    local_out = jnp.einsum("hlm,mhc->lhc", probs_b, values_h, preferred_element_type=jnp.float32)
    numer = jnp.einsum(
        "lhc,hcd->lhd", query_feat, memory, precision=precise, preferred_element_type=jnp.float32
    )
    denom = (
        jnp.einsum(
            "lhc,hc->lh",
            query_feat,
            memory_sum,
            precision=precise,
            preferred_element_type=jnp.float32,
        )
        + 1.0
    )
    mem_out = numer / denom[..., None]
    mixed = (
        (gate_mix * mem_out + (1.0 - gate_mix) * local_out)
        .astype(jnp.bfloat16)
        .reshape(length, width)
    )
    output = sent_and_summed(
        jnp.dot(mixed, out_weight, preferred_element_type=jnp.float32), "tp", 0
    ).astype(jnp.bfloat16)
    grad_mixed = lax.dot_general(
        gathered_copies(cotangent, "tp", 0),
        out_weight,
        (((1,), (1,)), ((), ())),
        preferred_element_type=jnp.float32,
    ).astype(jnp.bfloat16)
    grad_f = shaped(grad_mixed).astype(jnp.float32)
    grad_mem = gate_mix * grad_f
    grad_numer = grad_mem / denom[..., None]
    grad_denom = -jnp.sum(grad_mem * mem_out, -1) / denom
    memory_grad = jnp.einsum(
        "lhc,lhd->hcd",
        query_feat,
        grad_numer,
        precision=precise,
        preferred_element_type=jnp.float32,
    )
    sum_grad = jnp.einsum(
        "lh,lhc->hc", grad_denom, query_feat, precision=precise, preferred_element_type=jnp.float32
    )
    later_memory, later_sum = prefix_by_axis(
        (memory_grad, sum_grad),
        SEQ,
        add_pair,
        (jnp.zeros_like(memory_grad), jnp.zeros_like(sum_grad)),
        True,
    )
    grad_local = ((1.0 - gate_mix) * grad_f).astype(jnp.bfloat16)
    grad_probs = jnp.einsum(
        "lhc,mhc->hlm", grad_local, values_h, preferred_element_type=jnp.float32
    )
    delta = jnp.sum(probs * grad_probs, -1, keepdims=True)
    grad_scores = (probs * (grad_probs - delta) * scale_factor).astype(jnp.bfloat16)
    query_local = jnp.einsum(
        "hlm,mhc->lhc", grad_scores, keys_h, preferred_element_type=jnp.float32
    )
    keys_local = jnp.einsum(
        "hlm,lhc->mhc", grad_scores, query_h, preferred_element_type=jnp.float32
    )
    values_local = jnp.einsum(
        "hlm,lhc->mhc", probs_b, grad_local, preferred_element_type=jnp.float32
    )
    grad_qfeat = (
        jnp.einsum(
            "lhd,hcd->lhc",
            grad_numer,
            memory,
            precision=precise,
            preferred_element_type=jnp.float32,
        )
        + grad_denom[..., None] * memory_sum[None]
    )
    grad_kfeat = (
        jnp.einsum(
            "lhd,hcd->lhc",
            values_h,
            later_memory,
            precision=precise,
            preferred_element_type=jnp.float32,
        )
        + later_sum[None]
    )
    values_mem = jnp.einsum(
        "lhc,hcd->lhd",
        key_feat,
        later_memory,
        precision=precise,
        preferred_element_type=jnp.float32,
    )
    grad_query = (
        (query_local + grad_qfeat * slope_of(query_f)).astype(jnp.bfloat16).reshape(length, width)
    )
    grad_keys = (
        (keys_local + grad_kfeat * slope_of(keys_f)).astype(jnp.bfloat16).reshape(length, width)
    )
    grad_values = (values_local + values_mem).astype(jnp.bfloat16).reshape(length, width)
    return (output, grad_query, grad_keys, grad_values)


def solution(mesh):
    split = Mesh(mesh.devices.reshape(8, 4, 2, mesh.shape["tp"]), ("seq_0", "seq_1", "seq_2", "tp"))
    placed = (P(SEQ, "tp"), P(SEQ, "tp"), P(SEQ, "tp"), P("tp"), P("tp", None), P(SEQ_TP, None))
    return jax.shard_map(
        local,
        mesh=split,
        in_specs=placed,
        out_specs=(P(SEQ_TP, None), P(SEQ, "tp"), P(SEQ, "tp"), P(SEQ, "tp")),
        check_vma=False,
    )
```

profile of v0, /device:TPU:42, one launch (start us, length us, event | category | flops | bytes accessed | tf_op | source)
XLA Modules:
  0.0 179.4 jit_solution(10861451562746924583)
XLA Ops:
  7.2 2.8 %broadcast_in_dim.16 = bf16[4,128,2048]{2,1,0:T(8,128)(2,1)} broadcast(bf16[128,2048]{1,0:T(8,128)(2,1)} %param.11), dimensions={1,2} | broadcast | bytes 2621440 | tf_op jit(solution)/shard_map/broadcast_in_dim | solution.py:57
  10.0 4.9 %all-to-all-start.1 = ((bf16[4,128,2048]{2,1,0:T(8,128)(2,1)}), bf16[4,128,2048]{2,1,0:T(8,128)(2,1)}, u32[]{:S(2)}, u32[]{:S(2)}) async-start(bf16[4,128,2048]{2,1,0:T(8,128)(2,1)} %broadcast_in_dim.16), calls=%async_computation.1 | async-start | bytes 4194304 | tf_op jit(solution)/shard_map/all_to_all | solution.py:56
  17.5 2.0 %all-gather = bf16[8,128,128]{2,1,0:T(8,128)(2,1)S(1)} all-gather(bf16[4,128,128]{2,1,0:T(8,128)(2,1)S(1)} %convolution_convert_fusion.2), channel_id=2, replica_groups=mesh['seq_0'=8,'seq_1'=4,'seq_2'=2,'tp'=4] {'seq_2'}, dimensions={0}, use_global_device_ids=true | all-gather | bytes 393216 | tf_op jit(solution)/shard_map/all_gather | solution.py:27
  19.6 13.5 %all_gather.56 = bf16[4,4,128,128]{3,2,1,0:T(8,128)(2,1)S(1)} all-gather(bf16[1,4,128,128]{3,2,1,0:T(8,128)(2,1)S(1)} %fusion.128), channel_id=1, replica_groups=mesh['seq_0'=8,'seq_1'=4,'seq_2'=2,'tp'=4] {'seq_1'}, dimensions={0}, use_global_device_ids=true | all-gather | bytes 655360 | tf_op jit(solution)/shard_map/all_gather | solution.py:27
  36.0 7.1 %all_gather.59 = bf16[4,4,128]{2,1,0:T(4,128)(2,1)S(1)} all-gather(bf16[1,4,128]{2,1,0:T(4,128)(2,1)S(1)} %fusion.162), channel_id=1, replica_groups=mesh['seq_0'=8,'seq_1'=4,'seq_2'=2,'tp'=4] {'seq_1'}, dimensions={0}, use_global_device_ids=true | all-gather | bytes 5120 | tf_op jit(solution)/shard_map/all_gather | solution.py:27
  44.4 17.0 %all_gather.60 = bf16[8,4,128]{2,1,0:T(4,128)(2,1)S(1)} all-gather(bf16[1,4,128]{2,1,0:T(4,128)(2,1)S(1)} %fusion.161), channel_id=1, replica_groups=mesh['seq_0'=8,'seq_1'=4,'seq_2'=2,'tp'=4] {'seq_0'}, dimensions={0}, use_global_device_ids=true | all-gather | bytes 9216 | tf_op jit(solution)/shard_map/all_gather | solution.py:27
  62.8 4.7 %fusion.181 = (f32[4,512]{1,0:T(4,128)S(1)}, f32[4,512,512]{1,2,0:T(8,128)}) fusion(pred[512,512]{0,1:T(8,128)(4,1)} %iota_compare_fusion, bf16[512,4,128]{0,2,1:T(8,128)(2,1)S(1)} %bitcast.130, bf16[512,4,128]{0,2,1:T(8,128)(2,1)} %bitcast.124), kind=kOutput, calls=%fused_computation.223 | convolution fusion | flops 272630272 | bytes 5513216 | tf_op jit(solution)/shard_map/sub | solution.py:117
  67.5 2.9 %convolution_convert_fusion = bf16[512,512]{0,1:T(8,128)(2,1)S(1)} fusion(bf16[512,2048]{1,0:T(8,128)(2,1)} %bitcast.14, bf16[512,2048]{1,0:T(8,128)(2,1)S(1)} %copy-done), kind=kOutput, calls=%fused_computation.46 | convolution fusion | flops 1074003968 | bytes 4718592 | tf_op jit(solution)/shard_map/dot_general | solution.py:143
  71.4 2.1 %all-gather.1 = bf16[8,128,128]{2,1,0:T(8,128)(2,1)S(1)} all-gather(bf16[4,128,128]{2,1,0:T(8,128)(2,1)S(1)} %convolution_convert_fusion.1), channel_id=3, replica_groups=mesh['seq_0'=8,'seq_1'=4,'seq_2'=2,'tp'=4] {'seq_2'}, dimensions={0}, use_global_device_ids=true | all-gather | bytes 393216 | tf_op jit(solution)/shard_map/all_gather | solution.py:27
  74.3 13.0 %all_gather.63 = bf16[4,4,128,128]{3,2,1,0:T(8,128)(2,1)S(1)} all-gather(bf16[1,4,128,128]{3,2,1,0:T(8,128)(2,1)S(1)} %fusion.129), channel_id=1, replica_groups=mesh['seq_0'=8,'seq_1'=4,'seq_2'=2,'tp'=4] {'seq_1'}, dimensions={0}, use_global_device_ids=true | all-gather | bytes 655360 | tf_op jit(solution)/shard_map/all_gather | solution.py:27
  87.3 2.7 %fusion.65 = f32[4,512,512]{1,2,0:T(8,128)} fusion(bf16[512,4,128]{0,2,1:T(8,128)(2,1)S(1)} %bitcast.139, f32[4]{0:T(128)S(1)} %get-tuple-element.12, bf16[512,512]{1,0:T(8,128)(2,1)S(1)} %copy-done.8), kind=kOutput, calls=%fused_computation.72 | convolution fusion | flops 269221888 | bytes 5242896 | tf_op jit(solution)/shard_map/lhc,mhc->hlm/dot_general | solution.py:171
  90.0 1.8 %fusion.51 = f32[4,128,512]{2,1,0:T(8,128)} fusion(bf16[512,4,128]{0,2,1:T(8,128)(2,1)S(1)} %bitcast.140, f32[4]{0:T(128)S(1)} %get-tuple-element.12, f32[4,512,512]{1,2,0:T(8,128)S(1)} %copy-done.13, f32[4,512]{1,0:T(4,128)S(1)} %get-tuple-element.14), kind=kOutput, calls=%fused_computation.65 | convolution fusion | flops 271319040 | bytes 5775376 | tf_op jit(solution)/shard_map/hlm,lhc->mhc/dot_general | solution.py:182
  94.3 2.1 %fusion.40 = (f32[512,4]{0,1:T(4,128)S(1)}, f32[512,4,128]{0,2,1:T(8,128)S(1)}) fusion(f32[4]{0:T(128)S(1)} %get-tuple-element.13, bf16[512,512]{0,1:T(8,128)(2,1)} %copy-done.10, f32[512,4]{0,1:T(4,128)S(1)} %fusion.130, f32[4,128,128]{2,1,0:T(8,128)S(1)} %fusion.97, bf16[512,4,128]{0,2,1:T(8,128)(2,1)} %bitcast.132), kind=kOutput, calls=%fused_computation.54 | convolution fusion | flops 203945984 | bytes 2375696 | tf_op jit(solution)/shard_map/lhc,hcd->lhd/dot_general | solution.py:121
  98.9 3.3 %fusion.12 = f32[4,128,2048]{2,1,0:T(8,128)} fusion(bf16[512,2048]{1,0:T(8,128)(2,1)S(1)} %copy-done, bf16[4,128,512]{1,0,2:T(4,128)(2,1)S(1)} %dot_general.55), kind=kOutput, calls=%fused_computation.10 | convolution fusion | flops 1073741824 | bytes 6815744 | tf_op jit(solution)/shard_map/dot_general | solution.py:141
  102.2 4.9 %all-to-all-start = ((f32[4,128,2048]{2,1,0:T(8,128)}), f32[4,128,2048]{2,1,0:T(8,128)}, u32[]{:S(2)}, u32[]{:S(2)}) async-start(f32[4,128,2048]{2,1,0:T(8,128)} %fusion.12), calls=%async_computation | async-start | bytes 8388608 | tf_op jit(solution)/shard_map/all_to_all | solution.py:50
  108.1 8.6 %fusion.22 = f32[512,4,128]{0,2,1:T(8,128)} fusion(bf16[512,4,128]{0,2,1:T(8,128)(2,1)} %bitcast.133, f32[4,512,512]{1,2,0:T(8,128)} %fusion.65, f32[4,512,512]{1,2,0:T(8,128)} %get-tuple-element.15, f32[4,512]{1,0:T(4,128)S(1)} %get-tuple-element.14), kind=kOutput, calls=%fused_computation.28 | convolution fusion | flops 275778048 | bytes 9969664 | tf_op jit(solution)/shard_map/hlm,lhc->mhc/dot_general | solution.py:179
  116.7 8.8 %fusion.19 = f32[512,4,128]{0,2,1:T(8,128)} fusion(bf16[512,4,128]{0,2,1:T(8,128)(2,1)S(1)} %bitcast.125, f32[4,512,512]{1,2,0:T(8,128)} %fusion.65, f32[4,512,512]{1,2,0:T(8,128)} %get-tuple-element.15, f32[4,512]{1,0:T(4,128)S(1)} %get-tuple-element.14), kind=kOutput, calls=%fused_computation.27 | convolution fusion | flops 275778048 | bytes 9969664 | tf_op jit(solution)/shard_map/hlm,mhc->lhc/dot_general | solution.py:176
  125.5 3.5 %fusion.36 = bf16[512,4,128]{0,2,1:T(8,128)(2,1)} fusion(f32[512,4,128]{0,2,1:T(8,128)} %fusion.19, f32[4,128,128]{2,1,0:T(8,128)} %copy-done.11, bf16[512,4,128]{0,2,1:T(8,128)(2,1)} %bitcast.134, bf16[512,4,128]{0,2,1:T(8,128)(2,1)} %bitcast.141, f32[4,128]{1,0:T(4,128)S(1)} %bitcast.145, f32[512,4]{0,1:T(4,128)S(1)} %negate_divide_fusion, ...), kind=kOutput, calls=%fused_computation.48 | convolution fusion | flops 204472320 | bytes 2902032 | tf_op jit(solution)/shard_map/lhd,hcd->lhc/dot_general | solution.py:186
  128.9 2.0 %copy.55 = bf16[512,512]{1,0:T(8,128)(2,1)} copy(bf16[512,512]{0,1:T(8,128)(2,1)} %bitcast.136) | data formatting | bytes 1048576
  134.5 10.5 %all_gather.67 = bf16[4,4,128]{2,1,0:T(4,128)(2,1)S(1)} all-gather(bf16[1,4,128]{2,1,0:T(4,128)(2,1)S(1)} %fusion.159), channel_id=1, replica_groups=mesh['seq_0'=8,'seq_1'=4,'seq_2'=2,'tp'=4] {'seq_1'}, dimensions={0}, use_global_device_ids=true | all-gather | bytes 5120 | tf_op jit(solution)/shard_map/all_gather | solution.py:27
  144.9 15.5 %all_gather.68 = bf16[8,4,128]{2,1,0:T(4,128)(2,1)S(1)} all-gather(bf16[1,4,128]{2,1,0:T(4,128)(2,1)S(1)} %fusion.160), channel_id=1, replica_groups=mesh['seq_0'=8,'seq_1'=4,'seq_2'=2,'tp'=4] {'seq_0'}, dimensions={0}, use_global_device_ids=true | all-gather | bytes 9216 | tf_op jit(solution)/shard_map/all_gather | solution.py:27
  162.9 2.0 %fusion.35 = bf16[4,128,512]{2,1,0:T(8,128)(2,1)S(1)} fusion(f32[4,128,512]{2,1,0:T(8,128)} %fusion.51, f32[4,128,128]{2,1,0:T(8,128)S(1)} %fusion.110, bf16[512,4,128]{0,2,1:T(8,128)(2,1)S(1)} %bitcast.126), kind=kOutput, calls=%fused_computation.47 | convolution fusion | flops 203161600 | bytes 2359296 | tf_op jit(solution)/shard_map/lhc,hcd->lhd/dot_general | solution.py:205
  165.9 2.2 %fusion.37 = bf16[512,4,128]{0,2,1:T(8,128)(2,1)S(1)} fusion(f32[512,4,128]{0,2,1:T(8,128)} %fusion.22, f32[4,128,128]{2,1,0:T(8,128)} %copy-done.6, bf16[512,4,128]{0,2,1:T(8,128)(2,1)S(1)} %bitcast.127, f32[4,128]{1,0:T(4,128)S(1)} %fusion.150, bf16[512,512]{1,0:T(8,128)(2,1)} %param.8), kind=kOutput, calls=%fused_computation.49 | convolution fusion | flops 203423744 | bytes 2885632 | tf_op jit(solution)/shard_map/lhd,hcd->lhc/dot_general | solution.py:196
  169.1 3.4 %reduce_sum.47 = bf16[128,2048]{1,0:T(8,128)(2,1)} reduce(f32[4,128,2048]{2,1,0:T(8,128)} %all-to-all-done, f32[]{:T(128)} %constant.21.clone.1), dimensions={0}, to_apply=%region_3.4 | reduce | flops 786432 | bytes 4718596 | tf_op jit(solution)/shard_map/reduce_sum | solution.py:51
  (68 shorter events, 23.8 us)
Async XLA Ops:
  7.2 60.4 %copy-start = (bf16[512,2048]{1,0:T(8,128)(2,1)S(1)}, bf16[512,2048]{1,0:T(8,128)(2,1)}, u32[]{:S(2)}) copy-start(bf16[512,2048]{1,0:T(8,128)(2,1)} %param.10) | copy-start | bytes 6291460
  7.2 7.7 %copy-start.3 = (bf16[512,512]{1,0:T(8,128)(2,1)S(1)}, bf16[512,512]{1,0:T(8,128)(2,1)}, u32[]{:S(2)}) copy-start(bf16[512,512]{1,0:T(8,128)(2,1)} %param.7) | copy-start | bytes 1572868
  10.0 57.6 %all-to-all-start.1 = ((bf16[4,128,2048]{2,1,0:T(8,128)(2,1)}), bf16[4,128,2048]{2,1,0:T(8,128)(2,1)}, u32[]{:S(2)}, u32[]{:S(2)}) async-start(bf16[4,128,2048]{2,1,0:T(8,128)(2,1)} %broadcast_in_dim.16), calls=%async_computation.1 | async-start | bytes 4194304 | tf_op jit(solution)/shard_map/all_to_all | solution.py:56
  14.9 47.3 %copy-start.12 = (f32[4]{0:T(128)S(1)}, f32[4]{0:T(128)}, u32[]{:S(2)}) copy-start(f32[4]{0:T(128)} %param.9) | copy-start | bytes 52
  14.9 76.9 %all-gather.7.cloned.1.call-start = ((), (), s32[]{:S(2)}) async-start(), calls=%async_computation.2 | async-start | bytes 1179648 | tf_op jit(solution)/shard_map/all_gather | solution.py:27
  15.1 0.8 copy-start.4
  44.4 26.1 %copy-start.7 = (bf16[512,512]{0,1:T(8,128)(2,1)}, bf16[512,512]{0,1:T(8,128)(2,1)S(1)}, u32[]{:S(2)}) copy-start(bf16[512,512]{0,1:T(8,128)(2,1)S(1)} %copy.36) | copy-start | bytes 1572868
  70.4 19.5 %copy-start.10 = (bf16[512,512]{0,1:T(8,128)(2,1)}, bf16[512,512]{0,1:T(8,128)(2,1)S(1)}, u32[]{:S(2)}) copy-start(bf16[512,512]{0,1:T(8,128)(2,1)S(1)} %convolution_convert_fusion) | copy-start | bytes 1572868
  70.4 16.8 %copy-start.8 = (bf16[512,512]{1,0:T(8,128)(2,1)S(1)}, bf16[512,512]{1,0:T(8,128)(2,1)}, u32[]{:S(2)}) copy-start(bf16[512,512]{1,0:T(8,128)(2,1)} %param.8) | copy-start | bytes 1572868
  71.4 18.6 %copy-start.13 = (f32[4,512,512]{1,2,0:T(8,128)S(1)}, f32[4,512,512]{1,2,0:T(8,128)}, u32[]{:S(2)}) copy-start(f32[4,512,512]{1,2,0:T(8,128)} %get-tuple-element.15) | copy-start | bytes 12582916
  73.5 0.7 copy-start.1
  91.8 4.6 %copy-start.9 = (bf16[512,512]{1,0:T(8,128)(2,1)S(1)}, bf16[512,512]{1,0:T(8,128)(2,1)}, u32[]{:S(2)}) copy-start(bf16[512,512]{1,0:T(8,128)(2,1)} %param.8) | copy-start | bytes 1572868
  91.8 4.6 %copy-start.14 = (f32[4,512,512]{1,2,0:T(8,128)S(1)}, f32[4,512,512]{1,2,0:T(8,128)}, u32[]{:S(2)}) copy-start(f32[4,512,512]{1,2,0:T(8,128)} %get-tuple-element.15) | copy-start | bytes 12582916
  93.6 0.7 copy-start.11
  102.2 66.9 %all-to-all-start = ((f32[4,128,2048]{2,1,0:T(8,128)}), f32[4,128,2048]{2,1,0:T(8,128)}, u32[]{:S(2)}, u32[]{:S(2)}) async-start(f32[4,128,2048]{2,1,0:T(8,128)} %fusion.12), calls=%async_computation | async-start | bytes 8388608 | tf_op jit(solution)/shard_map/all_to_all | solution.py:50
  107.1 53.4 %all-gather.9.cloned.1.call-start = ((), (), s32[]{:S(2)}) async-start(), calls=%async_computation.3 | async-start | bytes 1179648 | tf_op jit(solution)/shard_map/all_gather | solution.py:27
  108.1 8.6 %copy-start.5 = (bf16[512,512]{0,1:T(8,128)(2,1)S(1)}, bf16[512,512]{0,1:T(8,128)(2,1)}, u32[]{:S(2)}) copy-start(bf16[512,512]{0,1:T(8,128)(2,1)} %copy-done.4) | copy-start | bytes 1572868
  125.4 35.1 %copy-start.2 = (bf16[8,128,128]{2,1,0:T(8,128)(2,1)S(1)}, bf16[8,128,128]{2,1,0:T(8,128)(2,1)}, u32[]{:S(2)}) copy-start(bf16[8,128,128]{2,1,0:T(8,128)(2,1)} %copy-done.1) | copy-start | bytes 786436
  162.2 0.7 copy-start.6
Sparse Core Ops, SparseCore 0:
  34.0 40.0 all-gather.6
  109.7 39.1 all-gather.8
where the time goes:
time: 180 us; the launch traced here: 179 us
  blocking collectives  84.3 us (47%)
  matrix products  48.6 us (27%)
  between operations  14.3 us (8%)
  local copies, waits for them, and re-layouts  12.4 us (7%)
  starting transfers between devices  10 us (6%)
  other arithmetic  9.57 us (5%)
    all_gather x10, blocking collectives, prefix_by_axis(): lax.all_gather(part.astype(kind), axis)  84.3 us
    dot_general x1, matrix products, local(): jnp.einsum('hlm,mhc->lhc', grad_scores, keys_h, preferred_element_type=jn...  8.75 us
    dot_general x1, matrix products, local(): jnp.einsum('hlm,lhc->mhc', grad_scores, query_h, preferred_element_type=j...  8.59 us
    unnamed x35, local copies, waits for them, and re-layouts  8.47 us
    all_to_all x1, starting transfers between devices, sent_to_all(): lax.all_to_all(jnp.broadcast_to(shard[None], (peers, *shard.shape)), axis...  4.91 us
    all_to_all x1, starting transfers between devices, sent_and_summed(): lax.all_to_all(cut_along(shard, dim, peers), axis, 0, 0, tiled=True)  4.89 us
    sub x1, matrix products, local(): expo = jnp.exp(scores - top_score)  4.74 us
  transfers between devices with their start and end apart: 4, of which 0 were waited for; matrix products, arithmetic and copies ran while one was open for 29% of the time, Pallas kernels for 0%

commit v1 on v0

v1 whole, which is shorter than its diff:
```python
import functools

import jax
import jax.numpy as jnp
from jax import lax
from jax.experimental import pallas as pl
from jax.experimental.pallas import tpu as pltpu
from jax.sharding import Mesh
from jax.sharding import PartitionSpec as P

HD = 128
SEQ = ("seq_0", "seq_1", "seq_2")
SEQ_TP = ("seq_0", "seq_1", "seq_2", "tp")
MESH = pl.DeviceIdType.MESH
F32 = jnp.float32
BF16 = jnp.bfloat16
BLOCK = 256
PAD = 16


def feat(x):
    return jnp.where(x > 0, x + 1.0, jnp.exp(jnp.minimum(x, 0.0)))


def slope(x):
    return jnp.where(x > 0, jnp.ones_like(x), jnp.exp(jnp.minimum(x, 0.0)))


def dot_nn(a, b):
    return jnp.dot(a, b, preferred_element_type=F32)


def dot_nt(a, b):
    return lax.dot_general(a, b, (((1,), (1,)), ((), ())), preferred_element_type=F32)


def dot_tn(a, b):
    return lax.dot_general(a, b, (((0,), (0,)), ((), ())), preferred_element_type=F32)


def kernel(
    zs, xs, cs, ts,
    q_in, k_in, v_in, beta, w_in, cot_in,
    out_o, gq_o, gk_o, gv_o,
    q_v, k_v, v_v, w_v, cot_v, load_sem,
    cot_send, cot_recv,
    parcel, got1, part, total, base, got2, back, got3,
    scan_send, scan_recv,
    probs, local_out, mem_out, rdenom, mixed, gm, kl, vl,
    pf, rs_src, rs_dst, rs_send, rs_recv,
    out_v, gq_v, gk_v, gv_v, store_sem,
):
    length, width = q_v.shape
    heads = width // HD
    rows = cot_in.shape[0]
    half = rows // 2
    group = xs * cs
    prow = parcel.shape[2] - PAD
    scale = HD ** (-0.5)

    z = lax.axis_index("seq_0")
    x = lax.axis_index("seq_1")
    c = lax.axis_index("seq_2")
    y = lax.axis_index("tp")
    g = x * cs + c
    right = lax.rem(y + 1, ts)
    left = lax.rem(y + ts - 1, ts)
    far = lax.rem(y + 2, ts)

    def at(x_=None, c_=None, z_=None, y_=None):
        return (
            z if z_ is None else z_,
            x if x_ is None else x_,
            c if c_ is None else c_,
            y if y_ is None else y_,
        )

    def member(p):
        return at(x_=p // cs, c_=lax.rem(p, cs))

    loads = []
    for i, (src, dst) in enumerate(
        ((k_in, k_v), (v_in, v_v), (q_in, q_v), (w_in, w_v), (cot_in, cot_v.at[y]))
    ):
        copy = pltpu.make_async_copy(src, dst, load_sem.at[i])
        copy.start()
        loads.append(copy)

    barrier = pltpu.get_barrier_semaphore()
    peers = [at(y_=left), at(y_=right)]
    peers += [member(lax.rem(g + d, group)) for d in range(1, group)]
    peers += [at(z_=lax.rem(z + d, zs)) for d in range(1, zs)]
    for peer in peers:
        pl.semaphore_signal(barrier, inc=1, device_id=peer, device_id_type=MESH)
    pl.semaphore_wait(barrier, len(peers))

    def remote(src, dst, send, recv, device):
        return pltpu.make_async_remote_copy(
            src_ref=src, dst_ref=dst, send_sem=send, recv_sem=recv,
            device_id=device, device_id_type=MESH,
        )

    first, second = pl.ds(0, half), pl.ds(half, half)

    def cot_copy(i, owner, part_, to, from_input):
        src = cot_in.at[part_] if from_input else cot_v.at[owner, part_]
        return remote(src, cot_v.at[owner, part_], cot_send.at[i], cot_recv.at[i], to)

    to_right, to_left = at(y_=right), at(y_=left)
    cot_out = [
        cot_copy(0, y, first, to_right, True),
        cot_copy(1, y, second, to_left, True),
        cot_copy(2, y, second, to_right, True),
        cot_copy(3, y, first, to_left, True),
        cot_copy(4, left, first, to_right, False),
        cot_copy(5, right, second, to_left, False),
    ]
    cot_arrive = [
        cot_copy(0, left, first, to_right, False),
        cot_copy(1, right, second, to_left, False),
        cot_copy(2, left, second, to_right, False),
        cot_copy(3, right, first, to_left, False),
        cot_copy(4, far, first, to_right, False),
        cot_copy(5, far, second, to_left, False),
    ]
    for i in range(4):
        cot_out[i].start()

    def cot_relay():
        for i in range(2):
            cot_arrive[i].wait_recv()
            cot_out[4 + i].start()

    def slices_out(s):
        return [
            remote(
                parcel.at[s, lax.rem(g + d, group)], got1.at[s, g],
                scan_send.at[s, 0, d], scan_recv.at[s, 0, d],
                member(lax.rem(g + d, group)),
            )
            for d in range(1, group)
        ]

    def slices_in(s):
        return [
            remote(
                parcel.at[s, g], got1.at[s, lax.rem(g + group - d, group)],
                scan_send.at[s, 0, d], scan_recv.at[s, 0, d],
                member(lax.rem(g + d, group)),
            )
            for d in range(1, group)
        ]

    def ahead(s, d):
        return z + d if s == 0 else z - d

    def behind(s, d):
        return z - d if s == 0 else z + d

    def inside(k):
        return jnp.logical_and(k >= 0, k < zs)

    def wrapped(k):
        return lax.rem(k + zs, zs)

    def total_out(s, d):
        return remote(
            total.at[s], got2.at[s, z], scan_send.at[s, 1, d], scan_recv.at[s, 1, d],
            at(z_=wrapped(ahead(s, d))),
        )

    def total_in(s, d):
        return remote(
            total.at[s], got2.at[s, wrapped(behind(s, d))],
            scan_send.at[s, 1, d], scan_recv.at[s, 1, d],
            at(z_=wrapped(ahead(s, d))),
        )

    def back_out(s):
        return [
            remote(
                back.at[s, lax.rem(g + d, group)], got3.at[s, g],
                scan_send.at[s, 2, d], scan_recv.at[s, 2, d],
                member(lax.rem(g + d, group)),
            )
            for d in range(1, group)
        ]

    def back_in(s):
        return [
            remote(
                back.at[s, g], got3.at[s, lax.rem(g + group - d, group)],
                scan_send.at[s, 2, d], scan_recv.at[s, 2, d],
                member(lax.rem(g + d, group)),
            )
            for d in range(1, group)
        ]

    def scan_put(s, h, memory, sums):
        wide = jnp.broadcast_to(sums, (PAD, HD)).astype(BF16)
        per = group // heads
        for j in range(per):
            parcel[s, h * per + j, 0:prow, :] = memory[j * prow : (j + 1) * prow].astype(BF16)
            parcel[s, h * per + j, prow : prow + PAD, :] = wide

    def scan_start(s):
        for copy in slices_out(s):
            copy.start()

    def scan_middle(s):
        got1[s, g] = parcel[s, g]
        for copy in slices_in(s):
            copy.wait_recv()
        run = jnp.zeros((prow + PAD, HD), F32)
        for p in range(group) if s == 0 else reversed(range(group)):
            part[p] = run
            run = run + got1[s, p].astype(F32)
        total[s] = run.astype(BF16)
        for d in range(1, zs):

            @pl.when(inside(ahead(s, d)))
            def _(d=d):
                total_out(s, d).start()

    def scan_back(s):
        base[...] = jnp.zeros_like(base)
        for d in range(1, zs):

            @pl.when(inside(behind(s, d)))
            def _(d=d):
                total_in(s, d).wait_recv()
                base[...] += got2[s, wrapped(behind(s, d))].astype(F32)

        for p in range(group):
            back[s, p] = (base[...] + part[p]).astype(BF16)
        got3[s, g] = back[s, g]
        for copy in back_out(s):
            copy.start()

    def scan_end(s):
        for copy in back_in(s):
            copy.wait_recv()

    def scan_get(s, h):
        per = group // heads
        memory = jnp.concatenate([got3[s, h * per + j, 0:prow, :] for j in range(per)], 0)
        sums = got3[s, h * per, prow : prow + PAD, :].astype(F32)[0:1]
        return memory, sums

    def scan_sent(s):
        for copy in slices_out(s):
            copy.wait_send()
        for d in range(1, zs):

            @pl.when(inside(ahead(s, d)))
            def _(d=d):
                total_out(s, d).wait_send()

        for copy in back_out(s):
            copy.wait_send()

    def cols(h):
        return pl.ds(h * HD, HD)

    def gate_of(h):
        return jax.nn.sigmoid(jnp.full((1, HD), beta[h], F32))

    blocks = length // BLOCK

    def attention(h):
        for i in range(blocks):
            q_rows, seen = pl.ds(i * BLOCK, BLOCK), pl.ds(0, (i + 1) * BLOCK)
            s_t = dot_nt(k_v[seen, cols(h)], q_v[q_rows, cols(h)]) * scale
            key_at = lax.broadcasted_iota(jnp.int32, s_t.shape, 0)
            query_at = lax.broadcasted_iota(jnp.int32, s_t.shape, 1) + i * BLOCK
            s_t = jnp.where(key_at <= query_at, s_t, -jnp.inf)
            e = jnp.exp(s_t - jnp.max(s_t, 0, keepdims=True))
            p = e * (1.0 / jnp.sum(e, 0, keepdims=True))
            probs[h, seen, q_rows] = p
            local_out[q_rows, cols(h)] = dot_tn(p.astype(BF16), v_v[seen, cols(h)])

    def attention_back(h):
        gate = gate_of(h)
        memory, sums = scan_get(0, h)
        for i in reversed(range(blocks)):
            q_rows, seen = pl.ds(i * BLOCK, BLOCK), pl.ds(0, (i + 1) * BLOCK)
            g_f = gm[q_rows, cols(h)].astype(F32)
            g_l = ((1.0 - gate) * g_f).astype(BF16)
            q_b = q_v[q_rows, cols(h)]
            p = probs[h, seen, q_rows]
            gp = dot_nt(v_v[seen, cols(h)], g_l)
            delta = jnp.sum(p * gp, 0, keepdims=True)
            gs = (p * (gp - delta) * scale).astype(BF16)
            k_add, v_add = dot_nn(gs, q_b), dot_nn(p.astype(BF16), g_l)
            if i == blocks - 1:
                kl[seen, cols(h)] = k_add
                vl[seen, cols(h)] = v_add
            else:
                kl[seen, cols(h)] += k_add
                vl[seen, cols(h)] += v_add
            g_m = gate * g_f
            rd = rdenom[h, q_rows, :]
            g_n = g_m * rd
            g_d = -jnp.sum(g_m * mem_out[q_rows, cols(h)], -1, keepdims=True) * rd
            g_q = dot_nt(g_n.astype(BF16), memory) + g_d * sums
            own = dot_tn(gs, k_v[seen, cols(h)])
            gq_v[q_rows, cols(h)] = (own + g_q * slope(q_b.astype(F32))).astype(BF16)

    loads[0].wait()
    loads[1].wait()
    for h in range(heads):
        kf = feat(k_v[:, cols(h)].astype(F32))
        scan_put(0, h, dot_tn(kf.astype(BF16), v_v[:, cols(h)]), jnp.sum(kf, 0, keepdims=True))
    scan_start(0)
    loads[2].wait()
    attention(0)
    scan_middle(0)
    attention(1)
    scan_back(0)
    cot_relay()
    for h in range(2, heads):
        attention(h)
    scan_end(0)

    for h in range(heads):
        gate = gate_of(h)
        memory, sums = scan_get(0, h)
        qf = feat(q_v[:, cols(h)].astype(F32))
        rd = 1.0 / (jnp.sum(qf * sums, -1, keepdims=True) + 1.0)
        rdenom[h] = rd
        m_o = dot_nn(qf.astype(BF16), memory) * rd
        mem_out[:, cols(h)] = m_o
        mixed[:, cols(h)] = (gate * m_o + (1.0 - gate) * local_out[:, cols(h)]).astype(BF16)

    loads[3].wait()
    loads[4].wait()

    def block_rows(b):
        return pl.ds(pl.multiple_of(b * rows, rows), rows)

    def project(b, slot):
        pf[slot] = dot_nn(mixed[block_rows(b), :], w_v[...])

    def rs_copy(i, to):
        return remote(rs_src.at[i], rs_dst.at[i], rs_send.at[i], rs_recv.at[i], to)

    rs = [rs_copy(i, to_right if i % 2 == 0 else to_left) for i in range(6)]

    def rs_start(i, piece):
        rs_src[i] = piece.astype(BF16)
        rs[i].start()

    project(far, 0)
    rs_start(0, pf[0, 0:half, :])
    rs_start(1, pf[0, half:rows, :])
    project(right, 1)
    rs_start(2, pf[1, half:rows, :])
    project(left, 2)
    rs_start(3, pf[2, 0:half, :])
    project(y, 3)

    def grad_in(b):
        gm[block_rows(b), :] = dot_nt(cot_v[b], w_v[...]).astype(BF16)

    grad_in(y)
    cot_arrive[2].wait_recv()
    grad_in(left)
    cot_arrive[3].wait_recv()
    grad_in(right)
    cot_arrive[4].wait_recv()
    cot_arrive[5].wait_recv()
    grad_in(far)

    for h in range(heads):
        qf = feat(q_v[:, cols(h)].astype(F32))
        g_m = gate_of(h) * gm[:, cols(h)].astype(F32)
        rd = rdenom[h]
        g_n = (g_m * rd).astype(BF16)
        g_d = -jnp.sum(g_m * mem_out[:, cols(h)], -1, keepdims=True) * rd
        scan_put(1, h, dot_tn(qf.astype(BF16), g_n), jnp.sum(g_d * qf, 0, keepdims=True))
    scan_start(1)
    attention_back(0)
    scan_middle(1)
    attention_back(1)
    scan_back(1)
    attention_back(2)
    rs[0].wait_recv()
    rs_start(4, pf[1, 0:half, :] + rs_dst[0].astype(F32))
    rs[1].wait_recv()
    rs_start(5, pf[2, half:rows, :] + rs_dst[1].astype(F32))
    attention_back(3)

    stores = [
        pltpu.make_async_copy(src, dst, store_sem.at[i])
        for i, (src, dst) in enumerate(
            ((gq_v, gq_o), (gk_v, gk_o), (gv_v, gv_o), (out_v, out_o))
        )
    ]
    stores[0].start()

    scan_end(1)
    for h in range(heads):
        memory, sums = scan_get(1, h)
        k_f = k_v[:, cols(h)].astype(F32)
        g_k = dot_nt(v_v[:, cols(h)], memory) + sums
        gk_v[:, cols(h)] = (kl[:, cols(h)] + g_k * slope(k_f)).astype(BF16)
        gv_v[:, cols(h)] = (vl[:, cols(h)] + dot_nn(feat(k_f).astype(BF16), memory)).astype(BF16)
    stores[1].start()
    stores[2].start()

    for i in range(2, 6):
        rs[i].wait_recv()
    out_v[0:half, :] = (
        pf[3, 0:half, :] + rs_dst[4].astype(F32) + rs_dst[3].astype(F32)
    ).astype(BF16)
    out_v[half:rows, :] = (
        pf[3, half:rows, :] + rs_dst[2].astype(F32) + rs_dst[5].astype(F32)
    ).astype(BF16)
    stores[3].start()

    for copy in cot_out:
        copy.wait_send()
    for copy in rs:
        copy.wait_send()
    scan_sent(0)
    scan_sent(1)
    for copy in stores:
        copy.wait()


def solution(mesh):
    split = Mesh(mesh.devices.reshape(8, 4, 2, mesh.shape["tp"]), SEQ_TP)
    zs, xs, cs, ts = split.devices.shape
    group = xs * cs

    def local(query, keys, values, beta, out_weight, cotangent):
        length, width = query.shape
        heads = width // HD
        rows, deep = cotangent.shape
        prow = heads * HD // group
        slab = prow + PAD
        vm = pltpu.VMEM
        dma = pltpu.SemaphoreType.DMA
        any_ = pl.BlockSpec(memory_space=pl.ANY)
        scratch = [
            vm((length, width), BF16), vm((length, width), BF16), vm((length, width), BF16),
            vm((width, deep), BF16), vm((ts, rows, deep), BF16), dma((5,)),
            dma((6,)), dma((6,)),
            vm((2, group, slab, HD), BF16), vm((2, group, slab, HD), BF16),
            vm((group, slab, HD), F32), vm((2, slab, HD), BF16), vm((slab, HD), F32),
            vm((2, zs, slab, HD), BF16),
            vm((2, group, slab, HD), BF16), vm((2, group, slab, HD), BF16),
            dma((2, 3, 8)), dma((2, 3, 8)),
            vm((heads, length, length), F32), vm((length, width), F32), vm((length, width), F32),
            vm((heads, length, 1), F32), vm((length, width), BF16), vm((length, width), BF16),
            vm((length, width), F32), vm((length, width), F32),
            vm((ts, rows, deep), F32), vm((6, rows // 2, deep), BF16), vm((6, rows // 2, deep), BF16),
            dma((6,)), dma((6,)),
            vm((rows, deep), BF16), vm((length, width), BF16), vm((length, width), BF16),
            vm((length, width), BF16), dma((4,)),
        ]
        return pl.pallas_call(
            functools.partial(kernel, zs, xs, cs, ts),
            out_shape=(
                jax.ShapeDtypeStruct((rows, deep), BF16),
                jax.ShapeDtypeStruct((length, width), BF16),
                jax.ShapeDtypeStruct((length, width), BF16),
                jax.ShapeDtypeStruct((length, width), BF16),
            ),
            in_specs=[any_, any_, any_, pl.BlockSpec(memory_space=pltpu.SMEM), any_, any_],
            out_specs=(any_, any_, any_, any_),
            scratch_shapes=scratch,
            compiler_params=pltpu.CompilerParams(
                collective_id=0, has_side_effects=True, vmem_limit_bytes=56 * 1024 * 1024
            ),
            cost_estimate=pl.CostEstimate(
                flops=5_000_000_000, bytes_accessed=8_000_000, transcendentals=2_000_000
            ),
            name="layer",
        )(query, keys, values, beta, out_weight, cotangent)

    placed = (P(SEQ, "tp"), P(SEQ, "tp"), P(SEQ, "tp"), P("tp"), P("tp", None), P(SEQ_TP, None))
    return jax.shard_map(
        local,
        mesh=split,
        in_specs=placed,
        out_specs=(P(SEQ_TP, None), P(SEQ, "tp"), P(SEQ, "tp"), P(SEQ, "tp")),
        check_vma=False,
    )
```

time: 180 us -> 61 us (0.34)
  the two profiles are of different devices: /device:TPU:42 before, /device:TPU:1 now
where the time goes in v1:
time: 61 us; the launch traced here: 60.9 us
  Pallas kernels  54.8 us (90%)
  local copies, waits for them, and re-layouts  5.43 us (9%)
  between operations  0.66 us (1%)
    pallas_call x1, Pallas kernels, local(): pl.pallas_call(functools.partial(kernel, zs, xs, cs, ts), out_shape=(jax....  54.8 us
    unnamed x8, local copies, waits for them, and re-layouts  5.43 us

profile of v1, /device:TPU:1, one launch (start us, length us, event | category | flops | bytes accessed | tf_op | source)
XLA Modules:
  0.0 60.9 jit_solution(3680296097786767291)
XLA Ops:
  0.6 54.8 %layer.1 = (bf16[128,2048]{1,0:T(8,128)(2,1)}, bf16[512,512]{1,0:T(8,128)(2,1)}, bf16[512,512]{1,0:T(8,128)(2,1)}, bf16[512,512]{1,0:T(8,128)(2,1)}) custom-call(bf16[512,512]{1,0:T(8,128)(2,1)} %q_in.1, bf16[512,512]{1,0:T(8,128)(2,1)} %k_in.1, bf16[512,512]{1,0:T(8,128)(2,1)} %v_in.1, f32[4]{0:T(128)} %beta.1, bf16[512,2048]{1,0:T(8,128)(2,1)} %w_in.1, ...), custom_call_target="tpu_custom_call" | custom-call | flops 5000000000 | bytes 8000000 | tf_op jit(solution)/shard_map/layer/pallas_call | solution.py:462
  55.4 0.0 copy-start.1
  55.4 0.0 copy-start
  55.4 2.0 %copy.14 = bf16[128,2048]{1,0:T(8,128)(2,1)} copy(bf16[128,2048]{1,0:T(8,128)(2,1)} %get-tuple-element.8) | data formatting | bytes 1048576
  57.4 1.9 %copy.15 = bf16[512,512]{1,0:T(8,128)(2,1)} copy(bf16[512,512]{1,0:T(8,128)(2,1)} %get-tuple-element.9) | data formatting | bytes 1048576
  59.3 0.0 copy-done.1
  59.3 0.8 %copy.16 = bf16[512,512]{1,0:T(8,128)(2,1)} copy(bf16[512,512]{1,0:T(8,128)(2,1)S(1)} %copy-done.1) | data formatting | bytes 1048576
  60.1 0.0 copy-done
  60.1 0.8 %copy.17 = bf16[512,512]{1,0:T(8,128)(2,1)} copy(bf16[512,512]{1,0:T(8,128)(2,1)S(1)} %copy-done) | data formatting | bytes 1048576
Async XLA Ops:
  55.4 3.9 %copy-start.1 = (bf16[512,512]{1,0:T(8,128)(2,1)S(1)}, bf16[512,512]{1,0:T(8,128)(2,1)}, u32[]{:S(2)}) copy-start(bf16[512,512]{1,0:T(8,128)(2,1)} %get-tuple-element.10) | copy-start | bytes 1572868
  55.4 4.6 %copy-start = (bf16[512,512]{1,0:T(8,128)(2,1)S(1)}, bf16[512,512]{1,0:T(8,128)(2,1)}, u32[]{:S(2)}) copy-start(bf16[512,512]{1,0:T(8,128)(2,1)} %get-tuple-element.11) | copy-start | bytes 1572868

commit v2 on v1

--- a/solution.py
+++ b/solution.py
@@ -41,14 +41,13 @@
 def kernel(
     zs, xs, cs, ts,
     q_in, k_in, v_in, beta, w_in, cot_in,
-    out_o, gq_o, gk_o, gv_o,
+    out_v, gq_v, gk_v, gv_v,
     q_v, k_v, v_v, w_v, cot_v, load_sem,
     cot_send, cot_recv,
     parcel, got1, part, total, base, got2, back, got3,
     scan_send, scan_recv,
     probs, local_out, mem_out, rdenom, mixed, gm, kl, vl,
     pf, rs_src, rs_dst, rs_send, rs_recv,
-    out_v, gq_v, gk_v, gv_v, store_sem,
 ):
     length, width = q_v.shape
     heads = width // HD
@@ -390,14 +389,6 @@
     rs_start(5, pf[2, half:rows, :] + rs_dst[1].astype(F32))
     attention_back(3)
 
-    stores = [
-        pltpu.make_async_copy(src, dst, store_sem.at[i])
-        for i, (src, dst) in enumerate(
-            ((gq_v, gq_o), (gk_v, gk_o), (gv_v, gv_o), (out_v, out_o))
-        )
-    ]
-    stores[0].start()
-
     scan_end(1)
     for h in range(heads):
         memory, sums = scan_get(1, h)
@@ -405,8 +396,6 @@
         g_k = dot_nt(v_v[:, cols(h)], memory) + sums
         gk_v[:, cols(h)] = (kl[:, cols(h)] + g_k * slope(k_f)).astype(BF16)
         gv_v[:, cols(h)] = (vl[:, cols(h)] + dot_nn(feat(k_f).astype(BF16), memory)).astype(BF16)
-    stores[1].start()
-    stores[2].start()
 
     for i in range(2, 6):
         rs[i].wait_recv()
@@ -416,7 +405,6 @@
     out_v[half:rows, :] = (
         pf[3, half:rows, :] + rs_dst[2].astype(F32) + rs_dst[5].astype(F32)
     ).astype(BF16)
-    stores[3].start()
 
     for copy in cot_out:
         copy.wait_send()
@@ -424,7 +412,17 @@
         copy.wait_send()
     scan_sent(0)
     scan_sent(1)
-    for copy in stores:
+
+
+def store(*refs):
+    sources, targets, sem = refs[:4], refs[4:8], refs[8]
+    copies = [
+        pltpu.make_async_copy(src, dst, sem.at[i])
+        for i, (src, dst) in enumerate(zip(sources, targets))
+    ]
+    for copy in copies:
+        copy.start()
+    for copy in copies:
         copy.wait()
 
 
@@ -456,28 +454,32 @@
             vm((length, width), F32), vm((length, width), F32),
             vm((ts, rows, deep), F32), vm((6, rows // 2, deep), BF16), vm((6, rows // 2, deep), BF16),
             dma((6,)), dma((6,)),
-            vm((rows, deep), BF16), vm((length, width), BF16), vm((length, width), BF16),
-            vm((length, width), BF16), dma((4,)),
         ]
-        return pl.pallas_call(
+        results = ((rows, deep), (length, width), (length, width), (length, width))
+        held = pl.pallas_call(
             functools.partial(kernel, zs, xs, cs, ts),
-            out_shape=(
-                jax.ShapeDtypeStruct((rows, deep), BF16),
-                jax.ShapeDtypeStruct((length, width), BF16),
-                jax.ShapeDtypeStruct((length, width), BF16),
-                jax.ShapeDtypeStruct((length, width), BF16),
-            ),
+            out_shape=tuple(vm(dims, BF16) for dims in results),
             in_specs=[any_, any_, any_, pl.BlockSpec(memory_space=pltpu.SMEM), any_, any_],
-            out_specs=(any_, any_, any_, any_),
+            out_specs=(pl.BlockSpec(memory_space=pltpu.VMEM),) * 4,
             scratch_shapes=scratch,
             compiler_params=pltpu.CompilerParams(
-                collective_id=0, has_side_effects=True, vmem_limit_bytes=56 * 1024 * 1024
+                collective_id=0, has_side_effects=True, vmem_limit_bytes=58 * 1024 * 1024
             ),
             cost_estimate=pl.CostEstimate(
                 flops=5_000_000_000, bytes_accessed=8_000_000, transcendentals=2_000_000
             ),
             name="layer",
         )(query, keys, values, beta, out_weight, cotangent)
+        return pl.pallas_call(
+            store,
+            out_shape=tuple(jax.ShapeDtypeStruct(dims, BF16) for dims in results),
+            in_specs=[any_] * 4,
+            out_specs=(any_,) * 4,
+            scratch_shapes=[dma((4,))],
+            compiler_params=pltpu.CompilerParams(vmem_limit_bytes=4 * 1024 * 1024),
+            cost_estimate=pl.CostEstimate(flops=0, bytes_accessed=4_000_000, transcendentals=0),
+            name="store",
+        )(*held)
 
     placed = (P(SEQ, "tp"), P(SEQ, "tp"), P(SEQ, "tp"), P("tp"), P("tp", None), P(SEQ_TP, None))
     return jax.shard_map(

time: 61 us -> 56.3 us (0.923)
  local copies, waits for them, and re-layouts: 5.43 us -> 0 us
    unnamed x8 -> x0, local copies, waits for them, and re-layouts: 5.43 us -> none
    pallas_call x1 -> x2, Pallas kernels: 54.8 us -> 55.4 us  [the longest x1 54 us: local(): pl.pallas_call(functools.partial(kernel, zs, xs, cs, ts), out_shape=tuple...]
where the time goes in v2:
time: 56.3 us; the launch traced here: 56.2 us
  Pallas kernels  55.4 us (98%)
  between operations  0.8 us (1%)
    pallas_call x1, Pallas kernels, local(): pl.pallas_call(functools.partial(kernel, zs, xs, cs, ts), out_shape=tuple...  54 us
    pallas_call x1, Pallas kernels, local(): pl.pallas_call(store, out_shape=tuple((jax.ShapeDtypeStruct(dims, BF16) f...  1.35 us

profile of v2, /device:TPU:1, one launch (start us, length us, event | category | flops | bytes accessed | tf_op | source)
XLA Modules:
  0.0 56.2 jit_solution(2103910061735463294)
XLA Ops:
  0.6 54.0 %layer.1 = (bf16[128,2048]{1,0:T(8,128)(2,1)S(1)}, bf16[512,512]{1,0:T(8,128)(2,1)S(1)}, bf16[512,512]{1,0:T(8,128)(2,1)S(1)}, bf16[512,512]{1,0:T(8,128)(2,1)S(1)}) custom-call(bf16[512,512]{1,0:T(8,128)(2,1)} %q_in.1, bf16[512,512]{1,0:T(8,128)(2,1)} %k_in.1, bf16[512,512]{1,0:T(8,128)(2,1)} %v_in.1, f32[4]{0:T(128)} %beta.1, bf16[512,2048]{1,0:T(8,128)(2,1)} %w_in.1, ...), custom_call_target="tpu_custom_call" | custom-call | flops 5000000000 | bytes 8000000 | tf_op jit(solution)/shard_map/layer/pallas_call | solution.py:459
  54.7 1.3 %store.1 = (bf16[128,2048]{1,0:T(8,128)(2,1)}, bf16[512,512]{1,0:T(8,128)(2,1)}, bf16[512,512]{1,0:T(8,128)(2,1)}, bf16[512,512]{1,0:T(8,128)(2,1)}) custom-call(bf16[128,2048]{1,0:T(8,128)(2,1)S(1)} %get-tuple-element.8.refs_0_, bf16[512,512]{1,0:T(8,128)(2,1)S(1)} %get-tuple-element.9.refs_1_, bf16[512,512]{1,0:T(8,128)(2,1)S(1)} %get-tuple-element.10.refs_2_, ...), custom_call_target="tpu_custom_call" | custom-call | bytes 4000000 | tf_op jit(solution)/shard_map/store/pallas_call | solution.py:473

commit v3 on v2

--- a/solution.py
+++ b/solution.py
@@ -312,13 +312,37 @@
         scan_put(0, h, dot_tn(kf.astype(BF16), v_v[:, cols(h)]), jnp.sum(kf, 0, keepdims=True))
     scan_start(0)
     loads[2].wait()
-    attention(0)
+    for h in range(heads):
+        attention(h)
     scan_middle(0)
-    attention(1)
+    cot_relay()
+
+    def block_rows(b):
+        return pl.ds(pl.multiple_of(b * rows, rows), rows)
+
+    def grad_in(b):
+        gm[block_rows(b), :] = dot_nt(cot_v[b], w_v[...]).astype(BF16)
+
+    def project(b, slot):
+        pf[slot] = dot_nn(mixed[block_rows(b), :], w_v[...])
+
+    def rs_copy(i, to):
+        return remote(rs_src.at[i], rs_dst.at[i], rs_send.at[i], rs_recv.at[i], to)
+
+    rs = [rs_copy(i, to_right if i % 2 == 0 else to_left) for i in range(6)]
+
+    def rs_start(i, piece):
+        rs_src[i] = piece.astype(BF16)
+        rs[i].start()
+
+    loads[3].wait()
+    loads[4].wait()
+    grad_in(y)
     scan_back(0)
-    cot_relay()
-    for h in range(2, heads):
-        attention(h)
+    cot_arrive[2].wait_recv()
+    grad_in(left)
+    cot_arrive[3].wait_recv()
+    grad_in(right)
     scan_end(0)
 
     for h in range(heads):
@@ -331,41 +355,9 @@
         mem_out[:, cols(h)] = m_o
         mixed[:, cols(h)] = (gate * m_o + (1.0 - gate) * local_out[:, cols(h)]).astype(BF16)
 
-    loads[3].wait()
-    loads[4].wait()
-
-    def block_rows(b):
-        return pl.ds(pl.multiple_of(b * rows, rows), rows)
-
-    def project(b, slot):
-        pf[slot] = dot_nn(mixed[block_rows(b), :], w_v[...])
-
-    def rs_copy(i, to):
-        return remote(rs_src.at[i], rs_dst.at[i], rs_send.at[i], rs_recv.at[i], to)
-
-    rs = [rs_copy(i, to_right if i % 2 == 0 else to_left) for i in range(6)]
-
-    def rs_start(i, piece):
-        rs_src[i] = piece.astype(BF16)
-        rs[i].start()
-
     project(far, 0)
     rs_start(0, pf[0, 0:half, :])
     rs_start(1, pf[0, half:rows, :])
-    project(right, 1)
-    rs_start(2, pf[1, half:rows, :])
-    project(left, 2)
-    rs_start(3, pf[2, 0:half, :])
-    project(y, 3)
-
-    def grad_in(b):
-        gm[block_rows(b), :] = dot_nt(cot_v[b], w_v[...]).astype(BF16)
-
-    grad_in(y)
-    cot_arrive[2].wait_recv()
-    grad_in(left)
-    cot_arrive[3].wait_recv()
-    grad_in(right)
     cot_arrive[4].wait_recv()
     cot_arrive[5].wait_recv()
     grad_in(far)
@@ -378,16 +370,21 @@
         g_d = -jnp.sum(g_m * mem_out[:, cols(h)], -1, keepdims=True) * rd
         scan_put(1, h, dot_tn(qf.astype(BF16), g_n), jnp.sum(g_d * qf, 0, keepdims=True))
     scan_start(1)
+    project(right, 1)
+    rs_start(2, pf[1, half:rows, :])
+    project(left, 2)
+    rs_start(3, pf[2, 0:half, :])
     attention_back(0)
+    attention_back(1)
     scan_middle(1)
-    attention_back(1)
-    scan_back(1)
+    project(y, 3)
     attention_back(2)
+    attention_back(3)
     rs[0].wait_recv()
     rs_start(4, pf[1, 0:half, :] + rs_dst[0].astype(F32))
     rs[1].wait_recv()
     rs_start(5, pf[2, half:rows, :] + rs_dst[1].astype(F32))
-    attention_back(3)
+    scan_back(1)
 
     scan_end(1)
     for h in range(heads):

time: 56.3 us -> 51.3 us (0.911)
  Pallas kernels: 55.4 us -> 50.6 us
    pallas_call x1, Pallas kernels: 54 us -> 49.2 us  [local(): pl.pallas_call(functools.partial(kernel, zs, xs, cs, ts), out_shape=tuple...]
where the time goes in v3:
time: 51.3 us; the launch traced here: 51.2 us
  Pallas kernels  50.6 us (99%)
  between operations  0.64 us (1%)
    pallas_call x1, Pallas kernels, local(): pl.pallas_call(functools.partial(kernel, zs, xs, cs, ts), out_shape=tuple...  49.2 us
    pallas_call x1, Pallas kernels, local(): pl.pallas_call(store, out_shape=tuple((jax.ShapeDtypeStruct(dims, BF16) f...  1.35 us

profile of v3, /device:TPU:1, one launch (start us, length us, event | category | flops | bytes accessed | tf_op | source)
XLA Modules:
  0.0 51.2 jit_solution(1120596245175033350)
XLA Ops:
  0.6 49.2 %layer.1 = (bf16[128,2048]{1,0:T(8,128)(2,1)S(1)}, bf16[512,512]{1,0:T(8,128)(2,1)S(1)}, bf16[512,512]{1,0:T(8,128)(2,1)S(1)}, bf16[512,512]{1,0:T(8,128)(2,1)S(1)}) custom-call(bf16[512,512]{1,0:T(8,128)(2,1)} %q_in.1, bf16[512,512]{1,0:T(8,128)(2,1)} %k_in.1, bf16[512,512]{1,0:T(8,128)(2,1)} %v_in.1, f32[4]{0:T(128)} %beta.1, bf16[512,2048]{1,0:T(8,128)(2,1)} %w_in.1, ...), custom_call_target="tpu_custom_call" | custom-call | flops 5000000000 | bytes 8000000 | tf_op jit(solution)/shard_map/layer/pallas_call | solution.py:456
  49.9 1.3 %store.1 = (bf16[128,2048]{1,0:T(8,128)(2,1)}, bf16[512,512]{1,0:T(8,128)(2,1)}, bf16[512,512]{1,0:T(8,128)(2,1)}, bf16[512,512]{1,0:T(8,128)(2,1)}) custom-call(bf16[128,2048]{1,0:T(8,128)(2,1)S(1)} %get-tuple-element.8.refs_0_, bf16[512,512]{1,0:T(8,128)(2,1)S(1)} %get-tuple-element.9.refs_1_, bf16[512,512]{1,0:T(8,128)(2,1)S(1)} %get-tuple-element.10.refs_2_, ...), custom_call_target="tpu_custom_call" | custom-call | bytes 4000000 | tf_op jit(solution)/shard_map/store/pallas_call | solution.py:470

commit v4 on v3

--- a/solution.py
+++ b/solution.py
@@ -18,12 +18,14 @@
 PAD = 16
 
 
-def feat(x):
-    return jnp.where(x > 0, x + 1.0, jnp.exp(jnp.minimum(x, 0.0)))
-
-
-def slope(x):
-    return jnp.where(x > 0, jnp.ones_like(x), jnp.exp(jnp.minimum(x, 0.0)))
+def feat_slope(x):
+    e = jnp.exp(jnp.minimum(x, 0.0))
+    return jnp.where(x > 0, x + 1.0, e), jnp.where(x > 0, jnp.ones_like(x), e)
+
+
+def by_distance(count, step):
+    hops = {d: min(d // step, count // step - d // step) for d in range(1, count)}
+    return sorted(hops, key=lambda d: -hops[d])
 
 
 def dot_nn(a, b):
@@ -44,9 +46,10 @@
     out_v, gq_v, gk_v, gv_v,
     q_v, k_v, v_v, w_v, cot_v, load_sem,
     cot_send, cot_recv,
-    parcel, got1, part, total, base, got2, back, got3,
+    parcel, got1, part, total, base, got2, back, got3, all_sums,
     scan_send, scan_recv,
     probs, local_out, mem_out, rdenom, mixed, gm, kl, vl,
+    kf_b, k_slope, q_feat, q_slope, grad_n, grad_d, grad_mem, grad_sum,
     pf, rs_src, rs_dst, rs_send, rs_recv,
 ):
     length, width = q_v.shape
@@ -91,7 +94,6 @@
     peers += [at(z_=lax.rem(z + d, zs)) for d in range(1, zs)]
     for peer in peers:
         pl.semaphore_signal(barrier, inc=1, device_id=peer, device_id_type=MESH)
-    pl.semaphore_wait(barrier, len(peers))
 
     def remote(src, dst, send, recv, device):
         return pltpu.make_async_remote_copy(
@@ -122,8 +124,6 @@
         cot_copy(4, far, first, to_right, False),
         cot_copy(5, far, second, to_left, False),
     ]
-    for i in range(4):
-        cot_out[i].start()
 
     def cot_relay():
         for i in range(2):
@@ -137,7 +137,7 @@
                 scan_send.at[s, 0, d], scan_recv.at[s, 0, d],
                 member(lax.rem(g + d, group)),
             )
-            for d in range(1, group)
+            for d in by_distance(group, cs)
         ]
 
     def slices_in(s):
@@ -147,7 +147,7 @@
                 scan_send.at[s, 0, d], scan_recv.at[s, 0, d],
                 member(lax.rem(g + d, group)),
             )
-            for d in range(1, group)
+            for d in by_distance(group, cs)
         ]
 
     def ahead(s, d):
@@ -182,7 +182,7 @@
                 scan_send.at[s, 2, d], scan_recv.at[s, 2, d],
                 member(lax.rem(g + d, group)),
             )
-            for d in range(1, group)
+            for d in by_distance(group, cs)
         ]
 
     def back_in(s):
@@ -192,15 +192,18 @@
                 scan_send.at[s, 2, d], scan_recv.at[s, 2, d],
                 member(lax.rem(g + d, group)),
             )
-            for d in range(1, group)
+            for d in by_distance(group, cs)
         ]
 
-    def scan_put(s, h, memory, sums):
-        wide = jnp.broadcast_to(sums, (PAD, HD)).astype(BF16)
+    def scan_put(s, memories, sums):
+        rest = jnp.zeros((PAD - heads, HD), F32)
+        wide = jnp.concatenate(sums + [rest], 0).astype(BF16)
         per = group // heads
-        for j in range(per):
-            parcel[s, h * per + j, 0:prow, :] = memory[j * prow : (j + 1) * prow].astype(BF16)
-            parcel[s, h * per + j, prow : prow + PAD, :] = wide
+        for h in range(heads):
+            for j in range(per):
+                piece = memories[h][j * prow : (j + 1) * prow]
+                parcel[s, h * per + j, 0:prow, :] = piece.astype(BF16)
+                parcel[s, h * per + j, prow : prow + PAD, :] = wide
 
     def scan_start(s):
         for copy in slices_out(s):
@@ -215,7 +218,7 @@
             part[p] = run
             run = run + got1[s, p].astype(F32)
         total[s] = run.astype(BF16)
-        for d in range(1, zs):
+        for d in by_distance(zs, 1):
 
             @pl.when(inside(ahead(s, d)))
             def _(d=d):
@@ -223,7 +226,7 @@
 
     def scan_back(s):
         base[...] = jnp.zeros_like(base)
-        for d in range(1, zs):
+        for d in by_distance(zs, 1):
 
             @pl.when(inside(behind(s, d)))
             def _(d=d):
@@ -231,25 +234,27 @@
                 base[...] += got2[s, wrapped(behind(s, d))].astype(F32)
 
         for p in range(group):
-            back[s, p] = (base[...] + part[p]).astype(BF16)
-        got3[s, g] = back[s, g]
+            back[s, p] = (base[0:prow, :] + part[p, 0:prow, :]).astype(BF16)
         for copy in back_out(s):
             copy.start()
+        got3[s, g] = back[s, g]
+        all_sums[s] = base[prow : prow + PAD, :] + part[g, prow : prow + PAD, :]
 
     def scan_end(s):
         for copy in back_in(s):
             copy.wait_recv()
 
-    def scan_get(s, h):
+    def scan_memory(s, h):
         per = group // heads
-        memory = jnp.concatenate([got3[s, h * per + j, 0:prow, :] for j in range(per)], 0)
-        sums = got3[s, h * per, prow : prow + PAD, :].astype(F32)[0:1]
-        return memory, sums
+        return jnp.concatenate([got3[s, h * per + j] for j in range(per)], 0)
+
+    def scan_sums(s, h):
+        return all_sums[s, h : h + 1, :]
 
     def scan_sent(s):
         for copy in slices_out(s):
             copy.wait_send()
-        for d in range(1, zs):
+        for d in by_distance(zs, 1):
 
             @pl.when(inside(ahead(s, d)))
             def _(d=d):
@@ -280,7 +285,7 @@
 
     def attention_back(h):
         gate = gate_of(h)
-        memory, sums = scan_get(0, h)
+        memory, sums = scan_memory(0, h), scan_sums(0, h)
         for i in reversed(range(blocks)):
             q_rows, seen = pl.ds(i * BLOCK, BLOCK), pl.ds(0, (i + 1) * BLOCK)
             g_f = gm[q_rows, cols(h)].astype(F32)
@@ -297,19 +302,23 @@
             else:
                 kl[seen, cols(h)] += k_add
                 vl[seen, cols(h)] += v_add
-            g_m = gate * g_f
-            rd = rdenom[h, q_rows, :]
-            g_n = g_m * rd
-            g_d = -jnp.sum(g_m * mem_out[q_rows, cols(h)], -1, keepdims=True) * rd
-            g_q = dot_nt(g_n.astype(BF16), memory) + g_d * sums
+            g_q = dot_nt(grad_n[q_rows, cols(h)], memory) + grad_d[h, q_rows, :] * sums
             own = dot_tn(gs, k_v[seen, cols(h)])
-            gq_v[q_rows, cols(h)] = (own + g_q * slope(q_b.astype(F32))).astype(BF16)
+            gq_v[q_rows, cols(h)] = (own + g_q * q_slope[q_rows, cols(h)]).astype(BF16)
 
     loads[0].wait()
     loads[1].wait()
+    memories, sums = [], []
     for h in range(heads):
-        kf = feat(k_v[:, cols(h)].astype(F32))
-        scan_put(0, h, dot_tn(kf.astype(BF16), v_v[:, cols(h)]), jnp.sum(kf, 0, keepdims=True))
+        kf, k_slope[:, cols(h)] = feat_slope(k_v[:, cols(h)].astype(F32))
+        kf_h = kf.astype(BF16)
+        kf_b[:, cols(h)] = kf_h
+        memories.append(dot_tn(kf_h, v_v[:, cols(h)]))
+        sums.append(jnp.sum(kf, 0, keepdims=True))
+    scan_put(0, memories, sums)
+    pl.semaphore_wait(barrier, len(peers))
+    for i in range(4):
+        cot_out[i].start()
     scan_start(0)
     loads[2].wait()
     for h in range(heads):
@@ -338,61 +347,91 @@
     loads[3].wait()
     loads[4].wait()
     grad_in(y)
+    for h in range(heads):
+        q_feat[:, cols(h)], q_slope[:, cols(h)] = feat_slope(q_v[:, cols(h)].astype(F32))
     scan_back(0)
+
+    for h in range(heads):
+        near = jnp.sum(q_feat[:, cols(h)] * scan_sums(0, h), -1, keepdims=True)
+        rdenom[h] = 1.0 / (near + 1.0)
+
+    def grad_block(b, start):
+        part_rows = block_rows(b)
+        for h in range(heads):
+            g_m = gate_of(h) * gm[part_rows, cols(h)].astype(F32)
+            g_n = (g_m * rdenom[h, part_rows, :]).astype(BF16)
+            grad_n[part_rows, cols(h)] = g_n
+            memory = dot_tn(q_feat[part_rows, cols(h)].astype(BF16), g_n)
+            grad_mem[h] = memory if start else grad_mem[h] + memory
+
+    def grad_row(b, start):
+        part_rows = block_rows(b)
+        for h in range(heads):
+            g_m = gate_of(h) * gm[part_rows, cols(h)].astype(F32)
+            over = jnp.sum(g_m * mem_out[part_rows, cols(h)], -1, keepdims=True)
+            g_d = -over * rdenom[h, part_rows, :]
+            grad_d[h, part_rows, :] = g_d
+            total_d = jnp.sum(g_d * q_feat[part_rows, cols(h)], 0, keepdims=True)
+            grad_sum[h] = total_d if start else grad_sum[h] + total_d
+
+    grad_block(y, True)
     cot_arrive[2].wait_recv()
     grad_in(left)
+    grad_block(left, False)
     cot_arrive[3].wait_recv()
     grad_in(right)
+    grad_block(right, False)
     scan_end(0)
 
-    for h in range(heads):
-        gate = gate_of(h)
-        memory, sums = scan_get(0, h)
-        qf = feat(q_v[:, cols(h)].astype(F32))
-        rd = 1.0 / (jnp.sum(qf * sums, -1, keepdims=True) + 1.0)
-        rdenom[h] = rd
-        m_o = dot_nn(qf.astype(BF16), memory) * rd
-        mem_out[:, cols(h)] = m_o
-        mixed[:, cols(h)] = (gate * m_o + (1.0 - gate) * local_out[:, cols(h)]).astype(BF16)
-
+    def read_block(b):
+        part_rows = block_rows(b)
+        for h in range(heads):
+            gate = gate_of(h)
+            q_b = q_feat[part_rows, cols(h)].astype(BF16)
+            m_o = dot_nn(q_b, scan_memory(0, h)) * rdenom[h, part_rows, :]
+            mem_out[part_rows, cols(h)] = m_o
+            mix = gate * m_o + (1.0 - gate) * local_out[part_rows, cols(h)]
+            mixed[part_rows, cols(h)] = mix.astype(BF16)
+
+    read_block(far)
     project(far, 0)
     rs_start(0, pf[0, 0:half, :])
     rs_start(1, pf[0, half:rows, :])
+    read_block(right)
+    project(right, 1)
+    rs_start(2, pf[1, half:rows, :])
+    read_block(left)
+    project(left, 2)
+    rs_start(3, pf[2, 0:half, :])
+    read_block(y)
+    grad_row(y, True)
+    grad_row(left, False)
+    grad_row(right, False)
     cot_arrive[4].wait_recv()
     cot_arrive[5].wait_recv()
     grad_in(far)
-
-    for h in range(heads):
-        qf = feat(q_v[:, cols(h)].astype(F32))
-        g_m = gate_of(h) * gm[:, cols(h)].astype(F32)
-        rd = rdenom[h]
-        g_n = (g_m * rd).astype(BF16)
-        g_d = -jnp.sum(g_m * mem_out[:, cols(h)], -1, keepdims=True) * rd
-        scan_put(1, h, dot_tn(qf.astype(BF16), g_n), jnp.sum(g_d * qf, 0, keepdims=True))
+    grad_block(far, False)
+    grad_row(far, False)
+    scan_put(1, [grad_mem[h] for h in range(heads)], [grad_sum[h] for h in range(heads)])
     scan_start(1)
-    project(right, 1)
-    rs_start(2, pf[1, half:rows, :])
-    project(left, 2)
-    rs_start(3, pf[2, 0:half, :])
     attention_back(0)
     attention_back(1)
     scan_middle(1)
-    project(y, 3)
-    attention_back(2)
-    attention_back(3)
     rs[0].wait_recv()
     rs_start(4, pf[1, 0:half, :] + rs_dst[0].astype(F32))
     rs[1].wait_recv()
     rs_start(5, pf[2, half:rows, :] + rs_dst[1].astype(F32))
+    project(y, 3)
+    attention_back(2)
+    attention_back(3)
     scan_back(1)
 
     scan_end(1)
     for h in range(heads):
-        memory, sums = scan_get(1, h)
-        k_f = k_v[:, cols(h)].astype(F32)
+        memory, sums = scan_memory(1, h), scan_sums(1, h)
         g_k = dot_nt(v_v[:, cols(h)], memory) + sums
-        gk_v[:, cols(h)] = (kl[:, cols(h)] + g_k * slope(k_f)).astype(BF16)
-        gv_v[:, cols(h)] = (vl[:, cols(h)] + dot_nn(feat(k_f).astype(BF16), memory)).astype(BF16)
+        gk_v[:, cols(h)] = (kl[:, cols(h)] + g_k * k_slope[:, cols(h)]).astype(BF16)
+        gv_v[:, cols(h)] = (vl[:, cols(h)] + dot_nn(kf_b[:, cols(h)], memory)).astype(BF16)
 
     for i in range(2, 6):
         rs[i].wait_recv()
@@ -444,11 +483,14 @@
             vm((2, group, slab, HD), BF16), vm((2, group, slab, HD), BF16),
             vm((group, slab, HD), F32), vm((2, slab, HD), BF16), vm((slab, HD), F32),
             vm((2, zs, slab, HD), BF16),
-            vm((2, group, slab, HD), BF16), vm((2, group, slab, HD), BF16),
+            vm((2, group, prow, HD), BF16), vm((2, group, prow, HD), BF16), vm((2, PAD, HD), F32),
             dma((2, 3, 8)), dma((2, 3, 8)),
             vm((heads, length, length), F32), vm((length, width), F32), vm((length, width), F32),
             vm((heads, length, 1), F32), vm((length, width), BF16), vm((length, width), BF16),
             vm((length, width), F32), vm((length, width), F32),
+            vm((length, width), BF16), vm((length, width), F32), vm((length, width), F32),
+            vm((length, width), F32), vm((length, width), BF16), vm((heads, length, 1), F32),
+            vm((heads, HD, HD), F32), vm((heads, 1, HD), F32),
             vm((ts, rows, deep), F32), vm((6, rows // 2, deep), BF16), vm((6, rows // 2, deep), BF16),
             dma((6,)), dma((6,)),
         ]

time: 51.3 us -> 50 us (0.975)
  Pallas kernels: 50.6 us -> 49.1 us
    pallas_call x1, Pallas kernels: 49.2 us -> 47.7 us  [local(): pl.pallas_call(functools.partial(kernel, zs, xs, cs, ts), out_shape=tuple...]
where the time goes in v4:
time: 50 us; the launch traced here: 49.9 us
  Pallas kernels  49.1 us (98%)
  between operations  0.8 us (2%)
    pallas_call x1, Pallas kernels, local(): pl.pallas_call(functools.partial(kernel, zs, xs, cs, ts), out_shape=tuple...  47.7 us
    pallas_call x1, Pallas kernels, local(): pl.pallas_call(store, out_shape=tuple((jax.ShapeDtypeStruct(dims, BF16) f...  1.35 us

profile of v4, /device:TPU:1, one launch (start us, length us, event | category | flops | bytes accessed | tf_op | source)
XLA Modules:
  0.0 49.9 jit_solution(10574147966471477696)
XLA Ops:
  0.6 47.7 %layer.1 = (bf16[128,2048]{1,0:T(8,128)(2,1)S(1)}, bf16[512,512]{1,0:T(8,128)(2,1)S(1)}, bf16[512,512]{1,0:T(8,128)(2,1)S(1)}, bf16[512,512]{1,0:T(8,128)(2,1)S(1)}) custom-call(bf16[512,512]{1,0:T(8,128)(2,1)} %q_in.1, bf16[512,512]{1,0:T(8,128)(2,1)} %k_in.1, bf16[512,512]{1,0:T(8,128)(2,1)} %v_in.1, f32[4]{0:T(128)} %beta.1, bf16[512,2048]{1,0:T(8,128)(2,1)} %w_in.1, ...), custom_call_target="tpu_custom_call" | custom-call | flops 5000000000 | bytes 8000000 | tf_op jit(solution)/shard_map/layer/pallas_call | solution.py:498
  48.4 1.3 %store.1 = (bf16[128,2048]{1,0:T(8,128)(2,1)}, bf16[512,512]{1,0:T(8,128)(2,1)}, bf16[512,512]{1,0:T(8,128)(2,1)}, bf16[512,512]{1,0:T(8,128)(2,1)}) custom-call(bf16[128,2048]{1,0:T(8,128)(2,1)S(1)} %get-tuple-element.8.refs_0_, bf16[512,512]{1,0:T(8,128)(2,1)S(1)} %get-tuple-element.9.refs_1_, bf16[512,512]{1,0:T(8,128)(2,1)S(1)} %get-tuple-element.10.refs_2_, ...), custom_call_target="tpu_custom_call" | custom-call | bytes 4000000 | tf_op jit(solution)/shard_map/store/pallas_call | solution.py:512

commit v5 on v4

--- a/solution.py
+++ b/solution.py
@@ -80,6 +80,13 @@
     def member(p):
         return at(x_=p // cs, c_=lax.rem(p, cs))
 
+    barrier = pltpu.get_barrier_semaphore()
+    peers = [at(z_=lax.rem(z + d, zs)) for d in by_distance(zs, 1)]
+    peers += [member(lax.rem(g + d, group)) for d in by_distance(group, cs)]
+    peers += [at(y_=left), at(y_=right)]
+    for peer in peers:
+        pl.semaphore_signal(barrier, inc=1, device_id=peer, device_id_type=MESH)
+
     loads = []
     for i, (src, dst) in enumerate(
         ((k_in, k_v), (v_in, v_v), (q_in, q_v), (w_in, w_v), (cot_in, cot_v.at[y]))
@@ -87,13 +94,6 @@
         copy = pltpu.make_async_copy(src, dst, load_sem.at[i])
         copy.start()
         loads.append(copy)
-
-    barrier = pltpu.get_barrier_semaphore()
-    peers = [at(y_=left), at(y_=right)]
-    peers += [member(lax.rem(g + d, group)) for d in range(1, group)]
-    peers += [at(z_=lax.rem(z + d, zs)) for d in range(1, zs)]
-    for peer in peers:
-        pl.semaphore_signal(barrier, inc=1, device_id=peer, device_id_type=MESH)
 
     def remote(src, dst, send, recv, device):
         return pltpu.make_async_remote_copy(
@@ -310,15 +310,16 @@
     loads[1].wait()
     memories, sums = [], []
     for h in range(heads):
+        if h == 2:
+            pl.semaphore_wait(barrier, len(peers))
+            for i in range(4):
+                cot_out[i].start()
         kf, k_slope[:, cols(h)] = feat_slope(k_v[:, cols(h)].astype(F32))
         kf_h = kf.astype(BF16)
         kf_b[:, cols(h)] = kf_h
         memories.append(dot_tn(kf_h, v_v[:, cols(h)]))
         sums.append(jnp.sum(kf, 0, keepdims=True))
     scan_put(0, memories, sums)
-    pl.semaphore_wait(barrier, len(peers))
-    for i in range(4):
-        cot_out[i].start()
     scan_start(0)
     loads[2].wait()
     for h in range(heads):
@@ -398,11 +399,7 @@
     rs_start(0, pf[0, 0:half, :])
     rs_start(1, pf[0, half:rows, :])
     read_block(right)
-    project(right, 1)
-    rs_start(2, pf[1, half:rows, :])
     read_block(left)
-    project(left, 2)
-    rs_start(3, pf[2, 0:half, :])
     read_block(y)
     grad_row(y, True)
     grad_row(left, False)
@@ -414,18 +411,21 @@
     grad_row(far, False)
     scan_put(1, [grad_mem[h] for h in range(heads)], [grad_sum[h] for h in range(heads)])
     scan_start(1)
+    project(right, 1)
+    rs_start(2, pf[1, half:rows, :])
+    project(left, 2)
+    rs_start(3, pf[2, 0:half, :])
     attention_back(0)
+    scan_middle(1)
     attention_back(1)
-    scan_middle(1)
+    attention_back(2)
     rs[0].wait_recv()
     rs_start(4, pf[1, 0:half, :] + rs_dst[0].astype(F32))
     rs[1].wait_recv()
     rs_start(5, pf[2, half:rows, :] + rs_dst[1].astype(F32))
+    scan_back(1)
+    attention_back(3)
     project(y, 3)
-    attention_back(2)
-    attention_back(3)
-    scan_back(1)
-
     scan_end(1)
     for h in range(heads):
         memory, sums = scan_memory(1, h), scan_sums(1, h)

time: 50 us -> 49.8 us (level)
  no operation moved by 1% of the time
where the time goes in v5:
time: 49.8 us; the launch traced here: 49.7 us
  Pallas kernels  49.1 us (99%)
  between operations  0.64 us (1%)
    pallas_call x1, Pallas kernels, local(): pl.pallas_call(functools.partial(kernel, zs, xs, cs, ts), out_shape=tuple...  47.7 us
    pallas_call x1, Pallas kernels, local(): pl.pallas_call(store, out_shape=tuple((jax.ShapeDtypeStruct(dims, BF16) f...  1.35 us

profile of v5, /device:TPU:1, one launch (start us, length us, event | category | flops | bytes accessed | tf_op | source)
XLA Modules:
  0.0 49.7 jit_solution(2873724856917711748)
XLA Ops:
  0.6 47.7 %layer.1 = (bf16[128,2048]{1,0:T(8,128)(2,1)S(1)}, bf16[512,512]{1,0:T(8,128)(2,1)S(1)}, bf16[512,512]{1,0:T(8,128)(2,1)S(1)}, bf16[512,512]{1,0:T(8,128)(2,1)S(1)}) custom-call(bf16[512,512]{1,0:T(8,128)(2,1)} %q_in.1, bf16[512,512]{1,0:T(8,128)(2,1)} %k_in.1, bf16[512,512]{1,0:T(8,128)(2,1)} %v_in.1, f32[4]{0:T(128)} %beta.1, bf16[512,2048]{1,0:T(8,128)(2,1)} %w_in.1, ...), custom_call_target="tpu_custom_call" | custom-call | flops 5000000000 | bytes 8000000 | tf_op jit(solution)/shard_map/layer/pallas_call | solution.py:498
  48.4 1.3 %store.1 = (bf16[128,2048]{1,0:T(8,128)(2,1)}, bf16[512,512]{1,0:T(8,128)(2,1)}, bf16[512,512]{1,0:T(8,128)(2,1)}, bf16[512,512]{1,0:T(8,128)(2,1)}) custom-call(bf16[128,2048]{1,0:T(8,128)(2,1)S(1)} %get-tuple-element.8.refs_0_, bf16[512,512]{1,0:T(8,128)(2,1)S(1)} %get-tuple-element.9.refs_1_, bf16[512,512]{1,0:T(8,128)(2,1)S(1)} %get-tuple-element.10.refs_2_, ...), custom_call_target="tpu_custom_call" | custom-call | bytes 4000000 | tf_op jit(solution)/shard_map/store/pallas_call | solution.py:512

commit v6 on v5

--- a/solution.py
+++ b/solution.py
@@ -426,13 +426,6 @@
     scan_back(1)
     attention_back(3)
     project(y, 3)
-    scan_end(1)
-    for h in range(heads):
-        memory, sums = scan_memory(1, h), scan_sums(1, h)
-        g_k = dot_nt(v_v[:, cols(h)], memory) + sums
-        gk_v[:, cols(h)] = (kl[:, cols(h)] + g_k * k_slope[:, cols(h)]).astype(BF16)
-        gv_v[:, cols(h)] = (vl[:, cols(h)] + dot_nn(kf_b[:, cols(h)], memory)).astype(BF16)
-
     for i in range(2, 6):
         rs[i].wait_recv()
     out_v[0:half, :] = (
@@ -441,6 +434,13 @@
     out_v[half:rows, :] = (
         pf[3, half:rows, :] + rs_dst[2].astype(F32) + rs_dst[5].astype(F32)
     ).astype(BF16)
+
+    scan_end(1)
+    for h in range(heads):
+        memory, sums = scan_memory(1, h), scan_sums(1, h)
+        g_k = dot_nt(v_v[:, cols(h)], memory) + sums
+        gk_v[:, cols(h)] = (kl[:, cols(h)] + g_k * k_slope[:, cols(h)]).astype(BF16)
+        gv_v[:, cols(h)] = (vl[:, cols(h)] + dot_nn(kf_b[:, cols(h)], memory)).astype(BF16)
 
     for copy in cot_out:
         copy.wait_send()

time: 49.8 us -> 50.3 us (1.010)
    pallas_call x1, Pallas kernels: 47.7 us -> 48.3 us  [local(): pl.pallas_call(functools.partial(kernel, zs, xs, cs, ts), out_shape=tuple...]
where the time goes in v6:
time: 50.3 us; the launch traced here: 50.2 us
  Pallas kernels  49.6 us (99%)
  between operations  0.64 us (1%)
    pallas_call x1, Pallas kernels, local(): pl.pallas_call(functools.partial(kernel, zs, xs, cs, ts), out_shape=tuple...  48.3 us
    pallas_call x1, Pallas kernels, local(): pl.pallas_call(store, out_shape=tuple((jax.ShapeDtypeStruct(dims, BF16) f...  1.35 us

profile of v6, /device:TPU:1, one launch (start us, length us, event | category | flops | bytes accessed | tf_op | source)
XLA Modules:
  0.0 50.2 jit_solution(17267393351168237969)
XLA Ops:
  0.6 48.3 %layer.1 = (bf16[128,2048]{1,0:T(8,128)(2,1)S(1)}, bf16[512,512]{1,0:T(8,128)(2,1)S(1)}, bf16[512,512]{1,0:T(8,128)(2,1)S(1)}, bf16[512,512]{1,0:T(8,128)(2,1)S(1)}) custom-call(bf16[512,512]{1,0:T(8,128)(2,1)} %q_in.1, bf16[512,512]{1,0:T(8,128)(2,1)} %k_in.1, bf16[512,512]{1,0:T(8,128)(2,1)} %v_in.1, f32[4]{0:T(128)} %beta.1, bf16[512,2048]{1,0:T(8,128)(2,1)} %w_in.1, ...), custom_call_target="tpu_custom_call" | custom-call | flops 5000000000 | bytes 8000000 | tf_op jit(solution)/shard_map/layer/pallas_call | solution.py:498
  48.9 1.3 %store.1 = (bf16[128,2048]{1,0:T(8,128)(2,1)}, bf16[512,512]{1,0:T(8,128)(2,1)}, bf16[512,512]{1,0:T(8,128)(2,1)}, bf16[512,512]{1,0:T(8,128)(2,1)}) custom-call(bf16[128,2048]{1,0:T(8,128)(2,1)S(1)} %get-tuple-element.8.refs_0_, bf16[512,512]{1,0:T(8,128)(2,1)S(1)} %get-tuple-element.9.refs_1_, bf16[512,512]{1,0:T(8,128)(2,1)S(1)} %get-tuple-element.10.refs_2_, ...), custom_call_target="tpu_custom_call" | custom-call | bytes 4000000 | tf_op jit(solution)/shard_map/store/pallas_call | solution.py:512
